TPU v7x, 512 devices: a whole 4x4x16 slice. The times are simulated.
512 devices in a mesh: tm: 16 (over x, y_hi, core), height: 16 (over z), mp: 2 (over y_lo).
Axes of the slice: x: 4, y: 4 (y_hi: 2, y_lo: 2; y = y_hi * 2 + y_lo), z: 16, core: 2. Of those that a mesh axis runs over, the one named last changes fastest.
Arguments:
- queries: bfloat16 [16, 16, 384, 1536], P('tm', 'height', None, 'mp'), may hold values from -6 to 6
- key_field: bfloat16 [16, 16, 384, 1536], P('tm', 'height', None, 'mp'), may hold values from -10 to 10
- value_field: bfloat16 [16, 16, 384, 1536], P('tm', 'height', None, 'mp'), may hold values from -6 to 6
- stream: bfloat16 [16, 16, 384, 3072], P('tm', 'height', None, 'mp'), may hold values from -3 to 3
- gate_scale: float32 [3072], P('mp'), may hold values from 0.5 to 1.5
- out_weight: bfloat16 [1536, 3072], P('height', 'mp'), may hold values from -0.15625 to 0.15625
- tile_lists: int32 [16, 16, 9], P('tm', 'height'), may hold values from -1 to 255, as said below
Outputs:
- block_out: bfloat16 [16, 16, 384, 3072], P('tm', 'height', None, 'mp')
Inputs may be any that keep to these rules, and one draw needn't show every extreme that they name: `tile_lists`: entry e names tile (e // 16, e % 16). The list of tile (a, b) names distinct tiles in increasing order, followed by -1 entries; they are all tiles of a box whose first indices form a run within a - 1 to a + 1 inside the same video (same a // 16) and whose second indices form a run within b - 1 to b + 1 inside the same column tile (same b // 16), and the box holds tile (a, b). Some list names 9 tiles and some list holds -1.
All inputs are finite; a program needn't handle non-finite values.
Results may differ from a plain program's by a relative error of at most 0.0059.
Values may be sent and summed in bfloat16 or wider, within the bound.
A program may use at most 128 MiB of HBM per device.

v0:
```python
import math

import jax
import jax.numpy as jnp
from jax import lax
from jax.sharding import PartitionSpec as P

HD = 128


def with_halo(cells, sides, width):
    for axis, dim in sides:
        count = lax.axis_size(axis)
        ends = count - 1
        head = lax.slice_in_dim(cells, 0, width, axis=dim)
        tail = lax.slice_in_dim(cells, cells.shape[dim] - width, cells.shape[dim], axis=dim)
        cells = jnp.concatenate(
            [
                lax.ppermute(tail, axis, [(i, (i + 1) % count) for i in range(ends)]),
                cells,
                lax.ppermute(head, axis, [((i + 1) % count, i) for i in range(ends)]),
            ],
            axis=dim,
        )
    return cells


def slot_mask(tile_lists, frame_index, row_index, frame_count, row_count):
    offsets = jnp.arange(3, dtype=jnp.int32) - 1
    slot_frames = frame_index + offsets[:, None]
    slot_rows = row_index + offsets[None, :]
    slot_ids = slot_frames * row_count + slot_rows
    inside = (
        (slot_frames >= 0)
        & (slot_frames < frame_count)
        & (slot_rows >= 0)
        & (slot_rows < row_count)
    )
    listed = tile_lists.reshape(-1)
    named = jnp.any(slot_ids[:, :, None] == listed[None, None, :], axis=2)
    return named & inside


def dense_heads(query_rows, beside_all, chosen, head_count):
    tokens = query_rows.shape[0]
    key_rows = beside_all[0].reshape(9 * tokens, -1)
    value_rows = beside_all[1].reshape(9 * tokens, -1)
    key_bias = jnp.where(jnp.repeat(chosen.reshape(9), tokens), 0.0, -jnp.inf).astype(jnp.float32)
    score_scale = 1.0 / math.sqrt(HD)
    outputs = []
    for head_index in range(head_count):
        lower = head_index * HD
        upper = lower + HD
        scores = (
            lax.dot_general(
                query_rows[:, lower:upper],
                key_rows[:, lower:upper],
                (((1,), (1,)), ((), ())),
                preferred_element_type=jnp.float32,
            )
            * score_scale
            + key_bias[None, :]
        )
        row_max = jnp.max(scores, axis=1, keepdims=True)
        weights = jnp.exp(scores - row_max).astype(jnp.bfloat16)
        total = jnp.sum(weights.astype(jnp.float32), axis=1, keepdims=True)
        outputs.append(
            jnp.dot(weights, value_rows[:, lower:upper], preferred_element_type=jnp.float32) / total
        )
    return jnp.concatenate(outputs, axis=1).astype(jnp.bfloat16)


def local(queries, key_field, value_field, stream, gate_scale, out_weight, tile_lists):
    groups_here, strips_here, cells_here, channels = queries.shape
    tokens = groups_here * strips_here * cells_here
    head_count = channels // HD
    query_rows = queries.reshape(tokens, channels)
    paired = jnp.stack(
        [key_field.reshape(tokens, channels), value_field.reshape(tokens, channels)]
    ).reshape(2, 1, 1, tokens, channels)
    beside_all = with_halo(paired, (("tm", 1), ("height", 2)), 1)
    frame_index = lax.axis_index("tm")
    row_index = lax.axis_index("height")
    frame_count = lax.axis_size("tm")
    row_count = lax.axis_size("height")
    chosen = slot_mask(tile_lists, frame_index, row_index, frame_count, row_count)
    attended = dense_heads(query_rows, beside_all, chosen, head_count)
    gathered = lax.all_gather(attended, "mp", axis=1, tiled=True)
    full_weight = lax.all_gather(out_weight, "height", axis=0, tiled=True)
    mixed = jnp.dot(gathered, full_weight, preferred_element_type=jnp.float32)
    result = stream.reshape(tokens, -1).astype(jnp.float32) + gate_scale[None, :] * mixed
    return result.astype(jnp.bfloat16).reshape(stream.shape)


def solution(mesh):
    placed = (
        P("tm", "height", None, "mp"),
        P("tm", "height", None, "mp"),
        P("tm", "height", None, "mp"),
        P("tm", "height", None, "mp"),
        P("mp"),
        P("height", "mp"),
        P("tm", "height", None),
    )
    return jax.shard_map(
        local, mesh=mesh, in_specs=placed, out_specs=P("tm", "height", None, "mp"), check_vma=False
    )
```

profile of v0, /device:TPU:14, one launch (start us, length us, event | category | flops | bytes accessed | tf_op | source)
XLA Modules:
  0.0 287.0 jit_solution(8467454233105034597)
XLA Ops:
  6.5 0.0 all-gather.3.cloned.1.call-start
  6.5 1.4 maximum_bitcast_fusion
  7.9 3.9 %collective-permute-start.1 = (bf16[2,1,1,384,768]{4,3,0,2,1:T(8,128)(2,1)S(1)}, bf16[2,1,1,384,768]{4,3,0,2,1:T(8,128)(2,1)S(1)}, u32[]{:S(2)}, u32[]{:S(2)}) collective-permute-start(bf16[2,1,1,384,768]{4,3,0,2,1:T(8,128)(2,1)S(1)} %maximum_bitcast_fusion), channel_id=1, source_target_pairs={{32,0},{64,32},{96,64},{128,96},{160,128},{192,160},{224,192},{256... | collective-permute-start | bytes 3538952 | tf_op jit(solution)/shard_map/ppermute | solution.py:21
  11.8 1.9 collective-permute-start
  13.7 11.8 %collective-permute-done.1 = bf16[2,1,1,384,768]{4,3,0,2,1:T(8,128)(2,1)S(1)} collective-permute-done((bf16[2,1,1,384,768]{4,3,0,2,1:T(8,128)(2,1)S(1)}, bf16[2,1,1,384,768]{4,3,0,2,1:T(8,128)(2,1)S(1)}, u32[]{:S(2)}, u32[]{:S(2)}) %collective-permute-start.1) | collective-permute-done | bytes 1179680 | tf_op jit(solution)/shard_map/ppermute | solution.py:21
  25.6 6.3 %collective-permute-done = bf16[2,1,1,384,768]{4,3,0,2,1:T(8,128)(2,1)S(1)} collective-permute-done((bf16[2,1,1,384,768]{4,3,0,2,1:T(8,128)(2,1)S(1)}, bf16[2,1,1,384,768]{4,3,0,2,1:T(8,128)(2,1)S(1)}, u32[]{:S(2)}, u32[]{:S(2)}) %collective-permute-start) | collective-permute-done | bytes 1179680 | tf_op jit(solution)/shard_map/ppermute | solution.py:19
  31.8 1.9 pad_maximum_fusion.1
  33.8 1.3 collective-permute-start.3
  35.1 6.3 %collective-permute-start.2 = (bf16[2,3,1,384,768]{4,3,0,2,1:T(8,128)(2,1)}, bf16[2,3,1,384,768]{4,3,0,2,1:T(8,128)(2,1)}, u32[]{:S(2)}, u32[]{:S(2)}) collective-permute-start(bf16[2,3,1,384,768]{4,3,0,2,1:T(8,128)(2,1)} %pad_maximum_fusion.1), channel_id=1, source_target_pairs={{0,2},{2,4},{4,6},{6,8},{8,10},{10,12},{12,14},{14,16},{16,18},{18... | collective-permute-start | bytes 10616840 | tf_op jit(solution)/shard_map/ppermute | solution.py:19
  41.4 0.1 broadcast_add_fusion
  41.5 0.0 copy-done.3
  41.5 0.2 compare_reduce_fusion
  41.7 0.1 and_select_fusion
  41.8 0.1 select_n.16
  41.9 0.7 broadcast_in_dim.12
  42.5 0.7 select_n.17
  43.3 65.3 %collective-permute-done.3 = bf16[2,3,1,384,768]{4,3,0,2,1:T(8,128)(2,1)} collective-permute-done((bf16[2,3,1,384,768]{4,3,0,2,1:T(8,128)(2,1)}, bf16[2,3,1,384,768]{4,3,0,2,1:T(8,128)(2,1)}, u32[]{:S(2)}, u32[]{:S(2)}) %collective-permute-start.3) | collective-permute-done | bytes 3538976 | tf_op jit(solution)/shard_map/ppermute | solution.py:21
  108.5 1.7 collective-permute-done.2
  110.3 8.2 %pad_maximum_fusion = bf16[2,3,3,384,768]{4,3,0,2,1:T(8,128)(2,1)} fusion(bf16[2,3,1,384,768]{4,3,0,2,1:T(8,128)(2,1)} %collective-permute-done.3, bf16[2,1,1,384,768]{4,3,0,2,1:T(8,128)(2,1)S(1)} %collective-permute-done.1, bf16[2,1,1,384,768]{4,3,0,2,1:T(8,128)(2,1)S(1)} %maximum_bitcast_fusion, bf16[2,1,1,384,768]{4,3,0,2,1:T(8,128)(2,1)S(1)} %collective-permute-done, ...), kind=kLoop, calls=%fused_computation | loop fusion | flops 21233664 | bytes 21233664 | tf_op jit(solution)/shard_map/concatenate | solution.py:17
  118.5 8.9 %fusion.42 = (bf16[1,3,3,384,768]{4,3,0,2,1:T(8,128)(2,1)}, bf16[1,3,3,384,768]{4,3,0,2,1:T(8,128)(2,1)}) fusion(bf16[2,3,3,384,768]{4,3,0,2,1:T(8,128)(2,1)} %pad_maximum_fusion), kind=kLoop, calls=%fused_computation.77 | loop fusion | bytes 21233664 | tf_op jit(solution)/shard_map/slice | solution.py:46
  127.4 3.2 %fusion.43 = (f32[384]{0:T(512)S(1)}, f32[3456,384]{1,0:T(8,128)S(1)}) fusion(f32[3456]{0:T(1024)S(1)} %select_n.17, bf16[384,768]{1,0:T(8,128)(2,1)S(1)} %bitcast.31, bf16[3456,768]{1,0:T(8,128)(2,1)} %bitcast.23), kind=kOutput, calls=%fused_computation.78 | convolution fusion | flops 343719552 | bytes 6309376 | tf_op jit(solution)/shard_map/dot_general | solution.py:55
  130.7 1.1 fusion.44
  131.7 1.0 fusion.45
  132.8 1.1 fusion.46
  133.8 1.1 fusion.47
  134.9 1.1 fusion.48
  136.0 0.8 convert_reduce_fusion.5
  136.8 0.9 fusion.10
  137.8 0.8 convert_reduce_fusion.4
  138.6 0.9 fusion.12
  139.5 0.8 convert_reduce_fusion.3
  140.4 1.0 fusion.14
  141.4 0.9 convert_reduce_fusion.2
  142.2 1.0 fusion.16
  143.2 1.1 convert_reduce_fusion.1
  144.2 0.9 fusion.18
  145.2 0.8 convert_reduce_fusion
  146.1 0.0 copy-start.5
  146.1 0.9 fusion.20
  147.0 0.0 copy-start.1
  147.0 0.8 copy-done.1
  147.8 0.0 all-gather.3.cloned.1.call-update
  147.9 0.0 all-gather.5.cloned.1.call-start
  147.9 0.7 all-gather.5.cloned.1.call-update
  148.6 41.7 %all-gather.3.cloned.1.call-done = bf16[384,1536]{1,0:T(8,128)(2,1)} async-done(((bf16[384,768]{1,0:T(8,128)(2,1)}), bf16[384,1536]{1,0:T(8,128)(2,1)}) %all-gather.3.cloned.1.call-update) | async-done | bytes 1179664 | tf_op jit(solution)/shard_map/all_gather | solution.py:88
  190.3 84.2 %all-gather.5.cloned.1.call-done = bf16[1536,1536]{1,0:T(8,128)(2,1)} async-done(((bf16[96,1536]{1,0:T(8,128)(2,1)}), bf16[1536,1536]{1,0:T(8,128)(2,1)}) %all-gather.5.cloned.1.call-update) | async-done | bytes 4718608 | tf_op jit(solution)/shard_map/all_gather | solution.py:89
  274.5 0.0 copy-done.4
  274.5 5.7 %fusion.8 = bf16[1,1,384,1536]{3,2,1,0:T(8,128)(2,1)} fusion(bf16[384,1536]{1,0:T(8,128)(2,1)} %all-gather.3.cloned.1.call-done, bf16[1536,1536]{1,0:T(8,128)(2,1)} %all-gather.5.cloned.1.call-done, bf16[1,1,384,1536]{3,2,1,0:T(8,128)(2,1)S(1)} %copy-done.4, f32[1536]{0:T(1024)S(1)} %copy-done.5), kind=kOutput, calls=%fused_computation.29 | convolution fusion | flops 1814298624 | bytes 8263680 | tf_op jit(solution)/shard_map/dot_general | solution.py:90
  (15 shorter events, 0.0 us)
Async XLA Ops:
  6.5 34.9 %copy-start.3 = (s32[1,1,9]{2,1,0:T(1,128)S(1)}, s32[1,1,9]{2,1,0:T(1,128)}, u32[]{:S(2)}) copy-start(s32[1,1,9]{2,1,0:T(1,128)} %param.13) | copy-start | bytes 112
  6.5 183.8 %all-gather.3.cloned.1.call-start = ((), (), s32[]{:S(2)}) async-start(), calls=%async_computation | async-start | bytes 1769472 | tf_op jit(solution)/shard_map/all_gather | solution.py:88
  7.9 17.7 %collective-permute-start.1 = (bf16[2,1,1,384,768]{4,3,0,2,1:T(8,128)(2,1)S(1)}, bf16[2,1,1,384,768]{4,3,0,2,1:T(8,128)(2,1)S(1)}, u32[]{:S(2)}, u32[]{:S(2)}) collective-permute-start(bf16[2,1,1,384,768]{4,3,0,2,1:T(8,128)(2,1)S(1)} %maximum_bitcast_fusion), channel_id=1, source_target_pairs={{32,0},{64,32},{96,64},{128,96},{160,128},{192,160},{224,192},{256... | collective-permute-start | bytes 3538952 | tf_op jit(solution)/shard_map/ppermute | solution.py:21
  11.8 20.0 %collective-permute-start = (bf16[2,1,1,384,768]{4,3,0,2,1:T(8,128)(2,1)S(1)}, bf16[2,1,1,384,768]{4,3,0,2,1:T(8,128)(2,1)S(1)}, u32[]{:S(2)}, u32[]{:S(2)}) collective-permute-start(bf16[2,1,1,384,768]{4,3,0,2,1:T(8,128)(2,1)S(1)} %maximum_bitcast_fusion), channel_id=1, source_target_pairs={{0,32},{32,64},{64,96},{96,128},{128,160},{160,192},{192,224},{224... | collective-permute-start | bytes 3538952 | tf_op jit(solution)/shard_map/ppermute | solution.py:19
  33.8 74.8 %collective-permute-start.3 = (bf16[2,3,1,384,768]{4,3,0,2,1:T(8,128)(2,1)}, bf16[2,3,1,384,768]{4,3,0,2,1:T(8,128)(2,1)}, u32[]{:S(2)}, u32[]{:S(2)}) collective-permute-start(bf16[2,3,1,384,768]{4,3,0,2,1:T(8,128)(2,1)} %pad_maximum_fusion.1), channel_id=1, source_target_pairs={{2,0},{4,2},{6,4},{8,6},{10,8},{12,10},{14,12},{16,14},{18,16},{20... | collective-permute-start | bytes 10616840 | tf_op jit(solution)/shard_map/ppermute | solution.py:21
  35.1 75.2 %collective-permute-start.2 = (bf16[2,3,1,384,768]{4,3,0,2,1:T(8,128)(2,1)}, bf16[2,3,1,384,768]{4,3,0,2,1:T(8,128)(2,1)}, u32[]{:S(2)}, u32[]{:S(2)}) collective-permute-start(bf16[2,3,1,384,768]{4,3,0,2,1:T(8,128)(2,1)} %pad_maximum_fusion.1), channel_id=1, source_target_pairs={{0,2},{2,4},{4,6},{6,8},{8,10},{10,12},{12,14},{14,16},{16,18},{18... | collective-permute-start | bytes 10616840 | tf_op jit(solution)/shard_map/ppermute | solution.py:19
  118.5 8.9 %copy-start.2 = (bf16[1,1,384,768]{3,2,1,0:T(8,128)(2,1)S(1)}, bf16[1,1,384,768]{3,2,1,0:T(8,128)(2,1)}, u32[]{:S(2)}) copy-start(bf16[1,1,384,768]{3,2,1,0:T(8,128)(2,1)} %param.7) | copy-start | bytes 1769476
  127.4 3.3 %copy-start = (bf16[1,3,3,384,768]{4,3,0,2,1:T(8,128)(2,1)S(1)}, bf16[1,3,3,384,768]{4,3,0,2,1:T(8,128)(2,1)}, u32[]{:S(2)}) copy-start(bf16[1,3,3,384,768]{4,3,0,2,1:T(8,128)(2,1)} %get-tuple-element.5) | copy-start | bytes 15925252
  133.8 3.0 %slice-start = ((s8[5308416]{0:T(1024)(128)(4,1)}), s8[4194304]{0:T(1024)(128)(4,1)S(1)}, s32[]{:S(2)}) async-start(s8[5308416]{0:T(1024)(128)(4,1)} %bitcast.15), calls=%async_computation.2 | async-start | bytes 8388608
  134.9 1.9 slice-start.1
  146.0 128.4 %copy-start.4 = (bf16[1,1,384,1536]{3,2,1,0:T(8,128)(2,1)S(1)}, bf16[1,1,384,1536]{3,2,1,0:T(8,128)(2,1)}, u32[]{:S(2)}) copy-start(bf16[1,1,384,1536]{3,2,1,0:T(8,128)(2,1)} %param.10) | copy-start | bytes 3538948
  146.1 128.4 %copy-start.5 = (f32[1536]{0:T(1024)S(1)}, f32[1536]{0:T(1024)}, u32[]{:S(2)}) copy-start(f32[1536]{0:T(1024)} %param.11) | copy-start | bytes 18436
  147.0 0.8 copy-start.1
  147.9 126.6 %all-gather.5.cloned.1.call-start = ((), (), s32[]{:S(2)}) async-start(), calls=%async_computation.1 | async-start | bytes 5013504 | tf_op jit(solution)/shard_map/all_gather | solution.py:89
Sparse Core Ops, SparseCore 0:
  148.0 42.2 all-gather.2
  192.4 82.0 all-gather.4
where the time goes:
time: 287 us
  waiting for transfers between devices  212 us (74%)
  matrix products  20 us (7%)
  other arithmetic  17.2 us (6%)
  starting transfers between devices  13.5 us (5%)
  between operations  13.5 us (5%)
  local copies, waits for them, and re-layouts  11.3 us (4%)
    all_gather x1, waiting for transfers between devices, local(): full_weight = lax.all_gather(out_weight, 'height', axis=0, tiled=True)  84.2 us
    ppermute x2, waiting for transfers between devices, with_halo(): lax.ppermute(head, axis, [((i + 1) % count, i) for i in range(ends)])  77.1 us
    all_gather x1, waiting for transfers between devices, local(): gathered = lax.all_gather(attended, 'mp', axis=1, tiled=True)  41.7 us
    concatenate x2, other arithmetic, with_halo(): jnp.concatenate([lax.ppermute(tail, axis, [(i, (i + 1) % count) for i in...  10.1 us
    slice x1, local copies, waits for them, and re-layouts, dense_heads(): key_rows = beside_all[0].reshape(9 * tokens, -1)  8.92 us
    dot_general x6, matrix products, dense_heads(): lax.dot_general(query_rows[:, lower:upper], key_rows[:, lower:upper], (((...  8.54 us
    ppermute x2, starting transfers between devices, with_halo(): lax.ppermute(tail, axis, [(i, (i + 1) % count) for i in range(ends)])  8.22 us
    ppermute x2, waiting for transfers between devices, with_halo(): lax.ppermute(tail, axis, [(i, (i + 1) % count) for i in range(ends)])  8.03 us
  transfers between devices with their start and end apart: 6, of which 6 were waited for; matrix products, arithmetic and copies ran while one was open for 1% of the time, Pallas kernels for 0%

commit v1 on v0

v1 whole, which is shorter than its diff:
```python
import math

import jax
import jax.numpy as jnp
from jax import lax
from jax.experimental import pallas as pl
from jax.experimental.pallas import tpu as pltpu
from jax.sharding import PartitionSpec as P

HD = 128
TOK = 384
G = 3
HALF = 768
OUT = 1536
PIECE = 48
COLS = 384
SUB = 128
FAR = 1e30
MESH = pl.DeviceIdType.MESH


def attend(hh, qbuf, kbuf, vbuf, flags, osend):
    scale = math.log2(math.e) / math.sqrt(HD)

    def block(sub, carry):
        rows = pl.ds(pl.multiple_of(sub * SUB, SUB), SUB)
        for j in range(2):
            q = qbuf[hh, j, rows, :]
            scores, tops, biases = [], [], []
            for r in range(3):
                for dt in range(3):
                    keys = kbuf[hh, r, (j + dt) * TOK:(j + dt + 1) * TOK, :]
                    s = lax.dot_general(
                        q, keys, (((1,), (1,)), ((), ())), preferred_element_type=jnp.float32
                    )
                    bias = flags[j, r * 3 + dt:r * 3 + dt + 1, 0:1]
                    scores.append(s)
                    biases.append(bias)
                    tops.append(jnp.max(s, axis=1, keepdims=True) - bias)
            top = tops[0]
            for t in tops[1:]:
                top = jnp.maximum(top, t)
            total = jnp.zeros((SUB, 1), jnp.float32)
            acc = jnp.zeros((SUB, HD), jnp.float32)
            for n in range(9):
                r, dt = divmod(n, 3)
                shift = (top + biases[n]) * scale
                w = jnp.exp2(scores[n] * scale - shift)
                total = total + jnp.sum(w, axis=1, keepdims=True)
                values = vbuf[hh, r, (j + dt) * TOK:(j + dt + 1) * TOK, :]
                acc = acc + jnp.dot(
                    w.astype(jnp.bfloat16), values, preferred_element_type=jnp.float32
                )
            osend[hh, j, rows, :] = (acc / total).astype(jnp.bfloat16)
        return carry

    lax.fori_loop(0, TOK // SUB, block, 0)


def weight_rows(wbuf, xp, start, count):
    parts = []
    row = start
    while row < start + count:
        z, rest = divmod(row, 2 * PIECE)
        c, low = divmod(rest, PIECE)
        high = min(PIECE, low + start + count - row)
        parts.append(wbuf[xp, z, c, low:high, :])
        row += high - low
    return jnp.concatenate(parts, axis=0)


def project(hh, oall, wbuf, acc):
    left = oall[hh]
    for xp in range(4):
        right = jnp.concatenate(
            [weight_rows(wbuf, xp, (g * G + hh) * HD, HD) for g in range(4)], axis=0
        )
        part = jnp.dot(left, right, preferred_element_type=jnp.float32)
        cols = slice(xp * COLS, (xp + 1) * COLS)
        if hh == 0:
            acc[:, cols] = part
        else:
            acc[:, cols] += part


def finish(acc, stream, gate, out):
    out[0, 0] = (stream[...].astype(jnp.float32) + gate[...] * acc[...]).astype(jnp.bfloat16)


def kernel(
    q_in, k_in, v_in, stream_in, gate, w_in, lists, out,
    qbuf, kbuf, vbuf, mine, flags, osend, oall, wbuf, stream, acc,
    ys, yr, zs, zr, qs, qr, os_, or_, fs, fr, wzs, wzr, wxs, wxr, wss, wsr, ls,
):
    tm, h, m = lax.axis_index("tm"), lax.axis_index("height"), lax.axis_index("mp")
    x, i = tm // 4, lax.rem(tm, 4)
    p, c = i // 2, lax.rem(i, 2)

    up = (tm, lax.rem(h + 1, 16), m)
    down = (tm, lax.rem(h + 15, 16), m)
    ring = 2 * x + c

    def on_ring(n):
        n = lax.rem(n + 8, 8)
        return ((n // 2) * 4 + 2 * p + lax.rem(n, 2), h, m)

    left, right = on_ring(ring - 1), on_ring(ring + 1)
    sibling = (tm + 1 - 2 * c, h, m)
    across = [(lax.rem(x + d, 4) * 4 + i, h, m) for d in (1, 2, 3)]
    homes = [(4 * x + 2 * j + p, h, 1 - m) for j in range(2)]
    outside = on_ring(ring - 1 + 2 * c)

    barrier = pltpu.get_barrier_semaphore()
    partners = [
        (4 * x + lax.rem(i + di, 4), h, lax.rem(m + dm, 2))
        for di in range(4) for dm in range(2) if (di, dm) != (0, 0)
    ] + [up, down, outside] + across
    for who in partners:
        pl.semaphore_signal(barrier, inc=1, device_id=who, device_id_type=MESH)

    for dz in range(3):
        for dt in range(3):
            frame, row = tm + dt - 1, h + dz - 1
            ident = frame * 16 + row
            hit = jnp.int32(0)
            for e in range(9):
                hit = hit | jnp.where(lists[0, 0, e] == ident, 1, 0)
            inside = (frame >= 0) & (frame < 16) & (row >= 0) & (row < 16)
            hit = jnp.where(inside, hit, 0)
            bias = jnp.where(hit > 0, jnp.float32(0.0), jnp.float32(FAR))
            n = dz * 3 + dt
            mine[n:n + 1, :] = jnp.full((1, HD), bias, jnp.float32)

    pl.semaphore_wait(barrier, len(partners))

    def remote(src, dst, send, recv, who):
        return pltpu.make_async_remote_copy(
            src_ref=src, dst_ref=dst, send_sem=send, recv_sem=recv, device_id=who, device_id_type=MESH
        )

    sent = []

    def start(copy):
        copy.start()
        sent.append(copy)

    sources = (k_in, v_in, q_in)

    def tile_slot(kind, hh, slot):
        if kind == 2:
            return qbuf.at[hh, slot]
        return (kbuf, vbuf)[kind].at[hh, 1, pl.ds(pl.multiple_of((1 + slot) * TOK, TOK), TOK), :]

    def y_copy(kind, hh, j, slot, recv_slot):
        return remote(
            sources[kind].at[0, 0, :, pl.ds((3 * j + hh) * HD, HD)],
            tile_slot(kind, hh, slot), ys.at[j, kind, hh], yr.at[recv_slot, kind, hh], homes[j],
        )

    own_rows = pl.ds(pl.multiple_of(PIECE * c, 16), PIECE)
    own_cols = pl.ds(pl.multiple_of(COLS * x, COLS), COLS)

    for hh in range(G):
        for kind in range(3):
            for j in range(2):
                start(y_copy(kind, hh, j, c, c))
        if hh == 0:
            for j in range(2):
                start(remote(mine, flags.at[c], fs.at[j], fr.at[c], homes[j]))

    def w_place(z):
        return wbuf.at[x, lax.rem(z + 32, 16), c]

    for way, who in ((0, up), (1, down)):
        start(remote(w_in.at[own_rows, own_cols], w_place(h), wzs.at[way, 0], wzr.at[way, 0], who))
    local = []
    for xp in range(4):
        local.append(pltpu.make_async_copy(
            w_in.at[own_rows, pl.ds(xp * COLS, COLS)], wbuf.at[xp, h, c], ls.at[xp]))
    local.append(pltpu.make_async_copy(stream_in.at[0, 0], stream, ls.at[4]))
    for copy in local:
        copy.start()

    def w_step(k):
        for way, who in ((0, up), (1, down)):
            if way == 1 and k == 8:
                continue
            z = h - k if way == 0 else h + k
            place = w_place(z)
            remote(place, place, wzs.at[way, k - 1], wzr.at[way, k - 1], who).wait_recv()
            if k < (8 if way == 0 else 7):
                start(remote(place, place, wzs.at[way, k], wzr.at[way, k], who))
            n = way * 8 + k - 1
            for d in range(3):
                start(remote(place, place, wxs.at[d, n], wxr.at[d, n], across[d]))

    def w_share():
        for xp in range(4):
            local[xp].wait()
        for d in range(3):
            src_x = lax.rem(x + 4 - (d + 1), 4)
            for n in range(15):
                z = h - (n + 1) if n < 8 else h + (n - 7)
                place = wbuf.at[src_x, lax.rem(z + 32, 16), c]
                remote(place, place, wxs.at[d, n], wxr.at[d, n], across[d]).wait_recv()
        for xp in range(4):
            start(remote(wbuf.at[xp, :, c], wbuf.at[xp, :, c], wss.at[xp], wsr.at[xp], sibling))

    def w_shared():
        for xp in range(4):
            remote(wbuf.at[xp, :, 1 - c], wbuf.at[xp, :, 1 - c], wss.at[xp], wsr.at[xp], sibling).wait_recv()

    def edge(kind, hh, r, col):
        return (kbuf, vbuf)[kind].at[hh, r, col * TOK:(col + 1) * TOK, :]

    def q_start(kind, hh, r):
        start(remote(edge(kind, hh, r, 2), edge(kind, hh, r, 0), qs.at[0, kind, hh, r], qr.at[0, kind, hh, r], right))
        start(remote(edge(kind, hh, r, 1), edge(kind, hh, r, 3), qs.at[1, kind, hh, r], qr.at[1, kind, hh, r], left))

    def q_wait(hh):
        for kind in range(2):
            for r in range(3):
                for way, col in ((0, 0), (1, 3)):
                    ref = edge(kind, hh, r, col)
                    remote(ref, ref, qs.at[way, kind, hh, r], qr.at[way, kind, hh, r], right).wait_recv()

    def pair(kind, hh, r):
        return (kbuf, vbuf)[kind].at[hh, r, TOK:3 * TOK, :]

    def own_ready(hh):
        for kind in range(2):
            for slot in range(2):
                y_copy(kind, hh, 0, slot, slot).wait_recv()
            for way, who in ((0, up), (1, down)):
                start(remote(pair(kind, hh, 1), pair(kind, hh, 2 * way),
                             zs.at[way, kind, hh], zr.at[way, kind, hh], who))
            q_start(kind, hh, 1)

    def rows_ready(hh):
        for kind in range(2):
            for way in range(2):
                ref = pair(kind, hh, 2 * way)
                remote(ref, ref, zs.at[way, kind, hh], zr.at[way, kind, hh], up).wait_recv()
                q_start(kind, hh, 2 * way)

    def queries_ready(hh):
        for slot in range(2):
            y_copy(2, hh, 0, slot, slot).wait_recv()
            if hh == 0:
                remote(mine, flags.at[slot], fs.at[0], fr.at[slot], homes[0]).wait_recv()

    group = 2 * (1 - m) + p

    def o_copies(hh, j, mm):
        who = (4 * x + 2 * c + j, h, jnp.int32(mm))
        here = (p == c) & (c == j) & (m == mm)
        dst = oall.at[hh, :, pl.ds(pl.multiple_of(group * HD, HD), HD)]
        src = osend.at[hh, j]
        far = remote(src, dst, os_.at[j, mm, hh], or_.at[group, hh], who)
        near = pltpu.make_async_copy(src, dst, or_.at[group, hh])
        return here, far, near

    def o_start(hh):
        for j in range(2):
            for mm in range(2):
                here, far, near = o_copies(hh, j, mm)
                pl.when(here)(near.start)
                pl.when(jnp.logical_not(here))(far.start)

    def o_wait(hh):
        for g in range(4):
            dst = oall.at[hh, :, g * HD:(g + 1) * HD]
            remote(dst, dst, os_.at[0, 0, hh], or_.at[g, hh], up).wait_recv()

    own_ready(0)
    w_step(1)
    own_ready(1)
    w_step(2)
    rows_ready(0)
    w_step(3)
    queries_ready(0)
    q_wait(0)
    attend(0, qbuf, kbuf, vbuf, flags, osend)
    o_start(0)
    own_ready(2)
    w_step(4)
    w_step(5)
    rows_ready(1)
    w_step(6)
    queries_ready(1)
    q_wait(1)
    attend(1, qbuf, kbuf, vbuf, flags, osend)
    o_start(1)
    w_step(7)
    w_step(8)
    rows_ready(2)
    queries_ready(2)
    w_share()
    q_wait(2)
    attend(2, qbuf, kbuf, vbuf, flags, osend)
    o_start(2)
    w_shared()
    for hh in range(G):
        o_wait(hh)
        project(hh, oall, wbuf, acc)
    local[4].wait()
    finish(acc, stream, gate, out)

    for copy in sent:
        copy.wait_send()
    for hh in range(G):
        for j in range(2):
            for mm in range(2):
                here, far, near = o_copies(hh, j, mm)
                pl.when(jnp.logical_not(here))(far.wait_send)


def local_call(queries, key_field, value_field, stream, gate_scale, out_weight, tile_lists):
    anywhere = pl.BlockSpec(memory_space=pl.ANY)
    vmem = pl.BlockSpec(memory_space=pltpu.VMEM)
    dma = pltpu.SemaphoreType.DMA
    return pl.pallas_call(
        kernel,
        out_shape=jax.ShapeDtypeStruct(stream.shape, jnp.bfloat16),
        in_specs=[anywhere] * 4 + [vmem, anywhere, pl.BlockSpec(memory_space=pltpu.SMEM)],
        out_specs=vmem,
        scratch_shapes=[
            pltpu.VMEM((G, 2, TOK, HD), jnp.bfloat16),
            pltpu.VMEM((G, 3, 4 * TOK, HD), jnp.bfloat16),
            pltpu.VMEM((G, 3, 4 * TOK, HD), jnp.bfloat16),
            pltpu.VMEM((16, HD), jnp.float32),
            pltpu.VMEM((2, 16, HD), jnp.float32),
            pltpu.VMEM((G, 2, TOK, HD), jnp.bfloat16),
            pltpu.VMEM((G, TOK, 4 * HD), jnp.bfloat16),
            pltpu.VMEM((4, 16, 2, PIECE, COLS), jnp.bfloat16),
            pltpu.VMEM((TOK, OUT), jnp.bfloat16),
            pltpu.VMEM((TOK, OUT), jnp.float32),
            dma((2, 3, G)), dma((2, 3, G)),
            dma((2, 2, G)), dma((2, 2, G)),
            dma((2, 2, G, 3)), dma((2, 2, G, 3)),
            dma((2, 2, G)), dma((4, G)),
            dma((2,)), dma((2,)),
            dma((2, 8)), dma((2, 8)),
            dma((3, 15)), dma((3, 15)),
            dma((4,)), dma((4,)),
            dma((5,)),
        ],
        compiler_params=pltpu.CompilerParams(
            collective_id=0, has_side_effects=True, vmem_limit_bytes=52 << 20
        ),
        name="block",
    )(queries, key_field, value_field, stream, gate_scale.reshape(1, OUT), out_weight, tile_lists)


def solution(mesh):
    placed = (
        P("tm", "height", None, "mp"),
        P("tm", "height", None, "mp"),
        P("tm", "height", None, "mp"),
        P("tm", "height", None, "mp"),
        P("mp"),
        P("height", "mp"),
        P("tm", "height", None),
    )
    return jax.shard_map(
        local_call, mesh=mesh, in_specs=placed, out_specs=P("tm", "height", None, "mp"), check_vma=False
    )
```

time: 287 us -> 112 us (0.39)
  the two profiles are of different devices: /device:TPU:14 before, /device:TPU:1 now
where the time goes in v1:
time: 112 us
  Pallas kernels  105 us (94%)
  local copies, waits for them, and re-layouts  6.8 us (6%)
    pallas_call x1, Pallas kernels, local_call(): pl.pallas_call(kernel, out_shape=jax.ShapeDtypeStruct(stream.shape, jnp.b...  105 us
    unnamed x9, local copies, waits for them, and re-layouts  6.1 us

profile of v1, /device:TPU:1, one launch (start us, length us, event | category | flops | bytes accessed | tf_op | source)
XLA Modules:
  0.0 112.1 jit_solution(14317018183364688551)
XLA Ops:
  0.0 0.7 reshape.3.gate
  0.7 0.0 copy-start
  0.7 1.1 copy-done
  1.8 0.0 copy-start.1
  1.8 1.1 copy-done.1
  2.8 0.0 copy-start.2
  2.8 1.0 copy-done.2
  3.8 0.0 copy-start.3
  3.8 0.7 copy-done.3
  4.4 105.3 %block.1 = bf16[1,1,384,1536]{3,2,1,0:T(8,128)(2,1)} custom-call(bf16[1,1,384,768]{3,2,1,0:T(8,128)(2,1)S(1)} %copy-done, bf16[1,1,384,768]{3,2,1,0:T(8,128)(2,1)S(1)} %copy-done.1, bf16[1,1,384,768]{3,2,1,0:T(8,128)(2,1)} %v_in.1, bf16[1,1,384,1536]{3,2,1,0:T(8,128)(2,1)} %stream_in.1, f32[1,1536]{1,0:T(1,128)S(1)} %reshape.3.gate, ...), custom_call_target="tpu_custom_call" | custom-call | tf_op jit(solution)/shard_map/block/pallas_call | solution.py:322
  109.8 2.4 %copy.9 = bf16[1,1,384,1536]{3,2,1,0:T(8,128)(2,1)} copy(bf16[1,1,384,1536]{3,2,1,0:T(8,128)(2,1)} %block.1) | data formatting | bytes 2359296
Async XLA Ops:
  0.7 1.1 copy-start
  1.8 1.1 copy-start.1
  2.8 1.0 copy-start.2
  3.8 0.7 copy-start.3

commit v2 on v1

v2 whole, which is shorter than its diff:
```python
import math

import jax
import jax.numpy as jnp
from jax import lax
from jax.experimental import pallas as pl
from jax.experimental.pallas import tpu as pltpu
from jax.sharding import PartitionSpec as P

HD = 128
TOK = 384
G = 3
HALF = 768
OUT = 1536
PIECE = 48
COLS = 768
SPAN = 384
FAR = 1e30
MESH = pl.DeviceIdType.MESH


def attend(hh, tiles, qbuf, kbuf, vbuf, flags, osend):
    scale = math.log2(math.e) / math.sqrt(HD)

    for j in tiles:
        q = qbuf[hh, j]
        window = slice(j * TOK, (j + 3) * TOK)
        bias = [jnp.broadcast_to(flags[j, n:n + 1, :], (TOK, HD)) for n in range(9)]
        scores = []
        for r in range(3):
            s = lax.dot_general(
                q, kbuf[hh, r, window, :], (((1,), (1,)), ((), ())), preferred_element_type=jnp.float32
            )
            scores += [s[:, g * HD:(g + 1) * HD] for g in range(9)]
        top = None
        for n in range(9):
            a = scores[3 * n:3 * n + 3]
            t = jnp.maximum(jnp.maximum(a[0], a[1]), a[2]) - bias[n]
            top = t if top is None else jnp.maximum(top, t)
        top = jnp.broadcast_to(jnp.max(top, axis=1, keepdims=True), (TOK, HD))
        total, acc = None, None
        for r in range(3):
            weights = []
            for n in range(3 * r, 3 * r + 3):
                shift = (top + bias[n]) * scale
                weights += [jnp.exp2(a * scale - shift) for a in scores[3 * n:3 * n + 3]]
            for w in weights:
                total = w if total is None else total + w
            part = jnp.dot(
                jnp.concatenate([w.astype(jnp.bfloat16) for w in weights], axis=1),
                vbuf[hh, r, window, :], preferred_element_type=jnp.float32,
            )
            acc = part if acc is None else acc + part
        total = jnp.broadcast_to(jnp.sum(total, axis=1, keepdims=True), (TOK, HD))
        osend[hh, j] = (acc / total).astype(jnp.bfloat16)


def weight_rows(wbuf, xp, cols, start, count):
    parts = []
    row = start
    while row < start + count:
        z, rest = divmod(row, 2 * PIECE)
        c, low = divmod(rest, PIECE)
        high = min(PIECE, low + start + count - row)
        parts.append(wbuf[xp, z, c, low:high, cols])
        row += high - low
    return jnp.concatenate(parts, axis=0)


def project(hh, oall, wbuf, acc):
    left = oall[hh]
    for n in range(OUT // SPAN):
        xp, low = divmod(n * SPAN, COLS)
        right = jnp.concatenate(
            [weight_rows(wbuf, xp, slice(low, low + SPAN), (g * G + hh) * HD, HD) for g in range(4)], axis=0
        )
        part = jnp.dot(left, right, preferred_element_type=jnp.float32)
        cols = slice(n * SPAN, (n + 1) * SPAN)
        if hh == 0:
            acc[:, cols] = part
        else:
            acc[:, cols] += part


def finish(acc, stream, gate, out):
    out[0, 0] = (stream[...].astype(jnp.float32) + gate[...].reshape(1, OUT) * acc[...]).astype(jnp.bfloat16)


def kernel(
    q_in, k_in, v_in, stream_in, gate_in, w_in, lists_in, out,
    lists, gate, qbuf, kbuf, vbuf, mine, flags, osend, oall, wbuf, stream, acc,
    ys, yr, zs, zr, qs, qr, os_, or_, fs, fr, wzs, wzr, wxs, wxr, wss, wsr, ls,
):
    tm, h, m = lax.axis_index("tm"), lax.axis_index("height"), lax.axis_index("mp")
    x, i = tm // 4, lax.rem(tm, 4)
    p, c = i // 2, lax.rem(i, 2)

    up = (tm, lax.rem(h + 1, 16), m)
    down = (tm, lax.rem(h + 15, 16), m)
    ring = 2 * x + c

    def on_ring(n):
        n = lax.rem(n + 8, 8)
        return ((n // 2) * 4 + 2 * p + lax.rem(n, 2), h, m)

    left, right = on_ring(ring - 1), on_ring(ring + 1)
    sibling = (tm + 1 - 2 * c, h, m)
    across = (lax.rem(x + 1 + 2 * c, 4) * 4 + i, h, m)
    back = (lax.rem(x + 3 - 2 * c, 4) * 4 + i, h, m)
    half = lax.rem(x, 2)
    homes = [(4 * x + 2 * j + p, h, 1 - m) for j in range(2)]
    outside = on_ring(ring - 1 + 2 * c)

    barrier = pltpu.get_barrier_semaphore()
    partners = [
        (4 * x + lax.rem(i + di, 4), h, lax.rem(m + dm, 2))
        for di in range(4) for dm in range(2) if (di, dm) != (0, 0)
    ] + [up, down, outside, across, back]
    for who in partners:
        pl.semaphore_signal(barrier, inc=1, device_id=who, device_id_type=MESH)

    named = pltpu.make_async_copy(lists_in, lists, ls.at[3])
    named.start()
    gates = pltpu.make_async_copy(gate_in, gate, ls.at[4])
    gates.start()
    named.wait()

    for dz in range(3):
        for dt in range(3):
            frame, row = tm + dt - 1, h + dz - 1
            ident = frame * 16 + row
            hit = jnp.int32(0)
            for e in range(9):
                hit = hit | jnp.where(lists[0, 0, e] == ident, 1, 0)
            inside = (frame >= 0) & (frame < 16) & (row >= 0) & (row < 16)
            hit = jnp.where(inside, hit, 0)
            bias = jnp.where(hit > 0, jnp.float32(0.0), jnp.float32(FAR))
            n = dz * 3 + dt
            mine[n:n + 1, :] = jnp.full((1, HD), bias, jnp.float32)

    pl.semaphore_wait(barrier, len(partners))

    def remote(src, dst, send, recv, who):
        return pltpu.make_async_remote_copy(
            src_ref=src, dst_ref=dst, send_sem=send, recv_sem=recv, device_id=who, device_id_type=MESH
        )

    sent = []

    def start(copy):
        copy.start()
        sent.append(copy)

    sources = (k_in, v_in, q_in)

    def tile_slot(kind, hh, slot):
        if kind == 2:
            return qbuf.at[hh, slot]
        return (kbuf, vbuf)[kind].at[hh, 1, pl.ds(pl.multiple_of((1 + slot) * TOK, TOK), TOK), :]

    def y_copy(kind, hh, j, slot, recv_slot):
        return remote(
            sources[kind].at[0, 0, :, pl.ds((3 * j + hh) * HD, HD)],
            tile_slot(kind, hh, slot), ys.at[j, kind, hh], yr.at[recv_slot, kind, hh], homes[j],
        )

    own_rows = pl.ds(pl.multiple_of(PIECE * c, 16), PIECE)
    own_cols = pl.ds(pl.multiple_of(COLS * half, COLS), COLS)

    for hh in range(G):
        for kind in range(3):
            for j in range(2):
                start(y_copy(kind, hh, j, c, c))
        if hh == 0:
            for j in range(2):
                start(remote(mine, flags.at[c], fs.at[j], fr.at[c], homes[j]))

    def w_place(z):
        return wbuf.at[half, lax.rem(z + 32, 16), c]

    for way, who in ((0, up), (1, down)):
        start(remote(w_in.at[own_rows, own_cols], w_place(h), wzs.at[way, 0], wzr.at[way, 0], who))
    local = []
    for xp in range(2):
        local.append(pltpu.make_async_copy(
            w_in.at[own_rows, pl.ds(xp * COLS, COLS)], wbuf.at[xp, h, c], ls.at[xp]))
    local.append(pltpu.make_async_copy(stream_in.at[0, 0], stream, ls.at[2]))
    for copy in local:
        copy.start()

    def w_step(k):
        for way, who in ((0, up), (1, down)):
            if way == 1 and k == 8:
                continue
            z = h - k if way == 0 else h + k
            place = w_place(z)
            remote(place, place, wzs.at[way, k - 1], wzr.at[way, k - 1], who).wait_recv()
            if k < (8 if way == 0 else 7):
                start(remote(place, place, wzs.at[way, k], wzr.at[way, k], who))
            n = way * 8 + k - 1
            start(remote(place, place, wxs.at[n], wxr.at[n], across))

    def share_own():
        for xp in range(2):
            local[xp].wait()
        place = wbuf.at[half, :, c]
        start(remote(place, place, wss.at[0], wsr.at[0], sibling))

    def share_other():
        for n in range(15):
            z = h - (n + 1) if n < 8 else h + (n - 7)
            place = wbuf.at[1 - half, lax.rem(z + 32, 16), c]
            remote(place, place, wxs.at[n], wxr.at[n], across).wait_recv()
        place = wbuf.at[1 - half, :, c]
        start(remote(place, place, wss.at[1], wsr.at[1], sibling))

    def w_shared():
        for n, which in ((0, half), (1, 1 - half)):
            place = wbuf.at[which, :, 1 - c]
            remote(place, place, wss.at[n], wsr.at[n], sibling).wait_recv()

    def edge(kind, hh, r, col):
        return (kbuf, vbuf)[kind].at[hh, r, col * TOK:(col + 1) * TOK, :]

    def q_start(kind, hh, r, slot):
        if slot == 1:
            start(remote(edge(kind, hh, r, 2), edge(kind, hh, r, 0), qs.at[0, kind, hh, r], qr.at[0, kind, hh, r], right))
        else:
            start(remote(edge(kind, hh, r, 1), edge(kind, hh, r, 3), qs.at[1, kind, hh, r], qr.at[1, kind, hh, r], left))

    def q_wait(hh):
        for kind in range(2):
            for r in range(3):
                for way, col in ((0, 0), (1, 3)):
                    ref = edge(kind, hh, r, col)
                    remote(ref, ref, qs.at[way, kind, hh, r], qr.at[way, kind, hh, r], right).wait_recv()

    def own_ready(hh, kind):
        for slot in range(2):
            y_copy(kind, hh, 0, slot, slot).wait_recv()

    def z_start(hh, kind, slot):
        for way, who in ((0, up), (1, down)):
            start(remote(edge(kind, hh, 1, 1 + slot), edge(kind, hh, 2 * way, 1 + slot),
                         zs.at[way, kind, hh, slot], zr.at[way, kind, hh, slot], who))
        q_start(kind, hh, 1, slot)

    def z_pass(hh, kind, slot):
        for way in range(2):
            ref = edge(kind, hh, 2 * way, 1 + slot)
            remote(ref, ref, zs.at[way, kind, hh, slot], zr.at[way, kind, hh, slot], up).wait_recv()
            q_start(kind, hh, 2 * way, slot)

    def queries_ready(hh):
        for slot in range(2):
            y_copy(2, hh, 0, slot, slot).wait_recv()
            if hh == 0:
                remote(mine, flags.at[slot], fs.at[0], fr.at[slot], homes[0]).wait_recv()

    group = 2 * (1 - m) + p

    def o_copies(hh, j, mm):
        who = (4 * x + 2 * c + j, h, jnp.int32(mm))
        here = (p == c) & (c == j) & (m == mm)
        dst = oall.at[hh, :, pl.ds(pl.multiple_of(group * HD, HD), HD)]
        src = osend.at[hh, j]
        far = remote(src, dst, os_.at[j, mm, hh], or_.at[group, hh], who)
        near = pltpu.make_async_copy(src, dst, or_.at[group, hh])
        return here, far, near

    def o_start(hh, tiles=(0, 1)):
        for j in tiles:
            for mm in range(2):
                here, far, near = o_copies(hh, j, mm)
                pl.when(here)(near.start)
                pl.when(jnp.logical_not(here))(far.start)

    def o_wait(hh):
        for g in range(4):
            dst = oall.at[hh, :, g * HD:(g + 1) * HD]
            remote(dst, dst, os_.at[0, 0, hh], or_.at[g, hh], up).wait_recv()

    def work(hh, tiles):
        attend(hh, tiles, qbuf, kbuf, vbuf, flags, osend)
        o_start(hh, tiles)

    def chunk(n):
        return n // 4, n // 2 % 2, n % 2

    def z_next(n):
        hh, kind, slot = chunk(n)
        if slot == 0:
            own_ready(hh, kind)
        z_start(hh, kind, slot)

    w_step(1)
    for n in range(6):
        z_next(n)
        w_step(n + 2)
        if n >= 2:
            z_pass(*chunk(n - 2))
    z_next(6)
    z_next(7)
    queries_ready(0)
    q_wait(0)
    work(0, (0, 1))
    w_step(8)
    z_pass(*chunk(4))
    z_next(8)
    z_next(9)
    share_own()
    z_pass(*chunk(5))
    z_next(10)
    z_next(11)
    z_pass(*chunk(6))
    z_pass(*chunk(7))
    queries_ready(1)
    q_wait(1)
    work(1, (0, 1))
    for n in range(8, 12):
        z_pass(*chunk(n))
    queries_ready(2)
    share_other()
    q_wait(2)
    work(2, (0,))
    work(2, (1,))
    w_shared()
    for hh in range(G):
        o_wait(hh)
        project(hh, oall, wbuf, acc)
    local[2].wait()
    gates.wait()
    finish(acc, stream, gate, out)

    for copy in sent:
        copy.wait_send()
    for hh in range(G):
        for j in range(2):
            for mm in range(2):
                here, far, near = o_copies(hh, j, mm)
                pl.when(jnp.logical_not(here))(far.wait_send)


def local_call(queries, key_field, value_field, stream, gate_scale, out_weight, tile_lists):
    hbm = pl.BlockSpec(memory_space=pltpu.HBM)
    vmem = pl.BlockSpec(memory_space=pltpu.VMEM)
    dma = pltpu.SemaphoreType.DMA
    return pl.pallas_call(
        kernel,
        out_shape=jax.ShapeDtypeStruct(stream.shape, jnp.bfloat16),
        in_specs=[hbm] * 7,
        out_specs=vmem,
        scratch_shapes=[
            pltpu.SMEM((1, 1, 9), jnp.int32),
            pltpu.VMEM((OUT,), jnp.float32),
            pltpu.VMEM((G, 2, TOK, HD), jnp.bfloat16),
            pltpu.VMEM((G, 3, 4 * TOK, HD), jnp.bfloat16),
            pltpu.VMEM((G, 3, 4 * TOK, HD), jnp.bfloat16),
            pltpu.VMEM((16, HD), jnp.float32),
            pltpu.VMEM((2, 16, HD), jnp.float32),
            pltpu.VMEM((G, 2, TOK, HD), jnp.bfloat16),
            pltpu.VMEM((G, TOK, 4 * HD), jnp.bfloat16),
            pltpu.VMEM((2, 16, 2, PIECE, COLS), jnp.bfloat16),
            pltpu.VMEM((TOK, OUT), jnp.bfloat16),
            pltpu.VMEM((TOK, OUT), jnp.float32),
            dma((2, 3, G)), dma((2, 3, G)),
            dma((2, 2, G, 2)), dma((2, 2, G, 2)),
            dma((2, 2, G, 3)), dma((2, 2, G, 3)),
            dma((2, 2, G)), dma((4, G)),
            dma((2,)), dma((2,)),
            dma((2, 8)), dma((2, 8)),
            dma((15,)), dma((15,)),
            dma((2,)), dma((2,)),
            dma((5,)),
        ],
        compiler_params=pltpu.CompilerParams(
            collective_id=0, has_side_effects=True, vmem_limit_bytes=63 << 20
        ),
        name="block",
    )(queries, key_field, value_field, stream, gate_scale, out_weight, tile_lists)


def solution(mesh):
    placed = (
        P("tm", "height", None, "mp"),
        P("tm", "height", None, "mp"),
        P("tm", "height", None, "mp"),
        P("tm", "height", None, "mp"),
        P("mp"),
        P("height", "mp"),
        P("tm", "height", None),
    )
    return jax.shard_map(
        local_call, mesh=mesh, in_specs=placed, out_specs=P("tm", "height", None, "mp"), check_vma=False
    )
```

time: 112 us -> 89.3 us (0.80)
  Pallas kernels: 105 us -> 86.7 us
  local copies, waits for them, and re-layouts: 6.8 us -> 2.36 us
    pallas_call x1, Pallas kernels: 105 us -> 86.7 us  [local_call(): pl.pallas_call(kernel, out_shape=jax.ShapeDtypeStruct(stream.shape, jnp.b...]
    unnamed x9 -> x1, local copies, waits for them, and re-layouts: 6.1 us -> 2.36 us
where the time goes in v2:
time: 89.3 us; the launch traced here: 89.1 us
  Pallas kernels  86.7 us (97%)
  local copies, waits for them, and re-layouts  2.36 us (3%)
    pallas_call x1, Pallas kernels, local_call(): pl.pallas_call(kernel, out_shape=jax.ShapeDtypeStruct(stream.shape, jnp.b...  86.7 us
    unnamed x1, local copies, waits for them, and re-layouts  2.36 us

profile of v2, /device:TPU:1, one launch (start us, length us, event | category | flops | bytes accessed | tf_op | source)
XLA Modules:
  0.0 89.1 jit_solution(16345327667347020341)
XLA Ops:
  0.0 86.7 %block.1 = bf16[1,1,384,1536]{3,2,1,0:T(8,128)(2,1)} custom-call(bf16[1,1,384,768]{3,2,1,0:T(8,128)(2,1)} %q_in.1, bf16[1,1,384,768]{3,2,1,0:T(8,128)(2,1)} %k_in.1, bf16[1,1,384,768]{3,2,1,0:T(8,128)(2,1)} %v_in.1, bf16[1,1,384,1536]{3,2,1,0:T(8,128)(2,1)} %stream_in.1, f32[1536]{0:T(1024)} %gate_in.1, bf16[96,1536]{1,0:T(8,128)(2,1)} %w_in.1, ...), custom_call_target="tpu_custom_call" | custom-call | tf_op jit(solution)/shard_map/block/pallas_call | solution.py:348
  86.7 2.4 %copy.9 = bf16[1,1,384,1536]{3,2,1,0:T(8,128)(2,1)} copy(bf16[1,1,384,1536]{3,2,1,0:T(8,128)(2,1)} %block.1) | data formatting | bytes 2359296

commit v3 on v2

--- a/solution.py
+++ b/solution.py
@@ -67,29 +67,22 @@
     return jnp.concatenate(parts, axis=0)
 
 
-def project(hh, oall, wbuf, acc):
-    left = oall[hh]
-    for n in range(OUT // SPAN):
-        xp, low = divmod(n * SPAN, COLS)
-        right = jnp.concatenate(
-            [weight_rows(wbuf, xp, slice(low, low + SPAN), (g * G + hh) * HD, HD) for g in range(4)], axis=0
-        )
-        part = jnp.dot(left, right, preferred_element_type=jnp.float32)
-        cols = slice(n * SPAN, (n + 1) * SPAN)
-        if hh == 0:
-            acc[:, cols] = part
-        else:
-            acc[:, cols] += part
-
-
-def finish(acc, stream, gate, out):
-    out[0, 0] = (stream[...].astype(jnp.float32) + gate[...].reshape(1, OUT) * acc[...]).astype(jnp.bfloat16)
+def project(heads, oall, wbuf, n):
+    xp, low = divmod(n * SPAN, COLS)
+    left = jnp.concatenate([oall[hh] for hh in heads], axis=1)
+    right = jnp.concatenate(
+        [
+            weight_rows(wbuf, xp, slice(low, low + SPAN), (g * G + hh) * HD, HD)
+            for hh in heads for g in range(4)
+        ], axis=0
+    )
+    return jnp.dot(left, right, preferred_element_type=jnp.float32)
 
 
 def kernel(
     q_in, k_in, v_in, stream_in, gate_in, w_in, lists_in, out,
-    lists, gate, qbuf, kbuf, vbuf, mine, flags, osend, oall, wbuf, stream, acc,
-    ys, yr, zs, zr, qs, qr, os_, or_, fs, fr, wzs, wzr, wxs, wxr, wss, wsr, ls,
+    lists, gate, qbuf, kbuf, vbuf, mine, flags, osend, oall, wbuf, stream, acc, result,
+    ys, yr, zs, zr, qs, qr, os_, or_, fs, fr, wzs, wzr, wxs, wxr, wss, wsr, ls, rs,
 ):
     tm, h, m = lax.axis_index("tm"), lax.axis_index("height"), lax.axis_index("mp")
     x, i = tm // 4, lax.rem(tm, 4)
@@ -294,43 +287,69 @@
         z_start(hh, kind, slot)
 
     w_step(1)
-    for n in range(6):
-        z_next(n)
-        w_step(n + 2)
-        if n >= 2:
-            z_pass(*chunk(n - 2))
+    z_next(0)
+    z_next(1)
+    w_step(2)
+    z_next(2)
+    z_next(3)
+    w_step(3)
+    z_pass(*chunk(0))
+    z_pass(*chunk(1))
+    z_next(4)
+    z_next(5)
+    w_step(4)
+    z_pass(*chunk(2))
+    z_pass(*chunk(3))
     z_next(6)
     z_next(7)
+    w_step(5)
+    z_pass(*chunk(4))
+    z_pass(*chunk(5))
+    z_next(8)
+    z_next(9)
     queries_ready(0)
     q_wait(0)
     work(0, (0, 1))
-    w_step(8)
-    z_pass(*chunk(4))
-    z_next(8)
-    z_next(9)
-    share_own()
-    z_pass(*chunk(5))
+    w_step(6)
+    z_pass(*chunk(6))
+    z_pass(*chunk(7))
     z_next(10)
     z_next(11)
-    z_pass(*chunk(6))
-    z_pass(*chunk(7))
+    w_step(7)
     queries_ready(1)
     q_wait(1)
     work(1, (0, 1))
-    for n in range(8, 12):
-        z_pass(*chunk(n))
+    z_pass(*chunk(8))
+    z_pass(*chunk(9))
+    w_step(8)
+    share_own()
+    z_pass(*chunk(10))
+    z_pass(*chunk(11))
+    share_other()
     queries_ready(2)
-    share_other()
     q_wait(2)
     work(2, (0,))
     work(2, (1,))
     w_shared()
-    for hh in range(G):
-        o_wait(hh)
-        project(hh, oall, wbuf, acc)
+    o_wait(0)
+    o_wait(1)
+    for n in range(OUT // SPAN):
+        acc[:, n * SPAN:(n + 1) * SPAN] = project((0, 1), oall, wbuf, n)
     local[2].wait()
     gates.wait()
-    finish(acc, stream, gate, out)
+    o_wait(2)
+    leaving = []
+    for n in range(OUT // SPAN):
+        cols = slice(n * SPAN, (n + 1) * SPAN)
+        mixed = acc[:, cols] + project((2,), oall, wbuf, n)
+        result[:, cols] = (
+            stream[:, cols].astype(jnp.float32) + gate[cols].reshape(1, SPAN) * mixed
+        ).astype(jnp.bfloat16)
+        copy = pltpu.make_async_copy(result.at[:, cols], out.at[0, 0, :, cols], rs.at[n])
+        copy.start()
+        leaving.append(copy)
+    for copy in leaving:
+        copy.wait()
 
     for copy in sent:
         copy.wait_send()
@@ -343,13 +362,12 @@
 
 def local_call(queries, key_field, value_field, stream, gate_scale, out_weight, tile_lists):
     hbm = pl.BlockSpec(memory_space=pltpu.HBM)
-    vmem = pl.BlockSpec(memory_space=pltpu.VMEM)
     dma = pltpu.SemaphoreType.DMA
     return pl.pallas_call(
         kernel,
         out_shape=jax.ShapeDtypeStruct(stream.shape, jnp.bfloat16),
         in_specs=[hbm] * 7,
-        out_specs=vmem,
+        out_specs=hbm,
         scratch_shapes=[
             pltpu.SMEM((1, 1, 9), jnp.int32),
             pltpu.VMEM((OUT,), jnp.float32),
@@ -363,6 +381,7 @@
             pltpu.VMEM((2, 16, 2, PIECE, COLS), jnp.bfloat16),
             pltpu.VMEM((TOK, OUT), jnp.bfloat16),
             pltpu.VMEM((TOK, OUT), jnp.float32),
+            pltpu.VMEM((TOK, OUT), jnp.bfloat16),
             dma((2, 3, G)), dma((2, 3, G)),
             dma((2, 2, G, 2)), dma((2, 2, G, 2)),
             dma((2, 2, G, 3)), dma((2, 2, G, 3)),
@@ -371,7 +390,7 @@
             dma((2, 8)), dma((2, 8)),
             dma((15,)), dma((15,)),
             dma((2,)), dma((2,)),
-            dma((5,)),
+            dma((5,)), dma((4,)),
         ],
         compiler_params=pltpu.CompilerParams(
             collective_id=0, has_side_effects=True, vmem_limit_bytes=63 << 20

time: 89.3 us -> 81 us (0.907)
  Pallas kernels: 86.7 us -> 78.4 us
    pallas_call x1, Pallas kernels: 86.7 us -> 78.4 us  [local_call(): pl.pallas_call(kernel, out_shape=jax.ShapeDtypeStruct(stream.shape, jnp.b...]
where the time goes in v3:
time: 81 us; the launch traced here: 80.8 us
  Pallas kernels  78.4 us (97%)
  local copies, waits for them, and re-layouts  2.36 us (3%)
    pallas_call x1, Pallas kernels, local_call(): pl.pallas_call(kernel, out_shape=jax.ShapeDtypeStruct(stream.shape, jnp.b...  78.4 us
    unnamed x1, local copies, waits for them, and re-layouts  2.36 us

profile of v3, /device:TPU:1, one launch (start us, length us, event | category | flops | bytes accessed | tf_op | source)
XLA Modules:
  0.0 80.8 jit_solution(9858115427622900806)
XLA Ops:
  0.0 78.4 %block.1 = bf16[1,1,384,1536]{3,2,1,0:T(8,128)(2,1)} custom-call(bf16[1,1,384,768]{3,2,1,0:T(8,128)(2,1)} %q_in.1, bf16[1,1,384,768]{3,2,1,0:T(8,128)(2,1)} %k_in.1, bf16[1,1,384,768]{3,2,1,0:T(8,128)(2,1)} %v_in.1, bf16[1,1,384,1536]{3,2,1,0:T(8,128)(2,1)} %stream_in.1, f32[1536]{0:T(1024)} %gate_in.1, bf16[96,1536]{1,0:T(8,128)(2,1)} %w_in.1, ...), custom_call_target="tpu_custom_call" | custom-call | tf_op jit(solution)/shard_map/block/pallas_call | solution.py:366
  78.4 2.4 %copy.9 = bf16[1,1,384,1536]{3,2,1,0:T(8,128)(2,1)} copy(bf16[1,1,384,1536]{3,2,1,0:T(8,128)(2,1)} %block.1) | data formatting | bytes 2359296

commit v4 on v3

--- a/solution.py
+++ b/solution.py
@@ -160,11 +160,10 @@
     own_rows = pl.ds(pl.multiple_of(PIECE * c, 16), PIECE)
     own_cols = pl.ds(pl.multiple_of(COLS * half, COLS), COLS)
 
-    for hh in range(G):
-        for kind in range(3):
-            for j in range(2):
-                start(y_copy(kind, hh, j, c, c))
-        if hh == 0:
+    for n, (kind, hh) in enumerate([(k, g) for g in range(G) for k in (0, 1)] + [(2, g) for g in range(G)]):
+        for j in range(2):
+            start(y_copy(kind, hh, j, c, c))
+        if n == 1:
             for j in range(2):
                 start(remote(mine, flags.at[c], fs.at[j], fr.at[c], homes[j]))
 

time: 81 us -> 81 us (level)
  no operation moved by 1% of the time
where the time goes in v4:
time: 81 us; the launch traced here: 80.8 us
  Pallas kernels  78.4 us (97%)
  local copies, waits for them, and re-layouts  2.36 us (3%)
    pallas_call x1, Pallas kernels, local_call(): pl.pallas_call(kernel, out_shape=jax.ShapeDtypeStruct(stream.shape, jnp.b...  78.4 us
    unnamed x1, local copies, waits for them, and re-layouts  2.36 us

profile of v4, /device:TPU:1, one launch (start us, length us, event | category | flops | bytes accessed | tf_op | source)
XLA Modules:
  0.0 80.8 jit_solution(332039286962801364)
XLA Ops:
  0.0 78.4 %block.1 = bf16[1,1,384,1536]{3,2,1,0:T(8,128)(2,1)} custom-call(bf16[1,1,384,768]{3,2,1,0:T(8,128)(2,1)} %q_in.1, bf16[1,1,384,768]{3,2,1,0:T(8,128)(2,1)} %k_in.1, bf16[1,1,384,768]{3,2,1,0:T(8,128)(2,1)} %v_in.1, bf16[1,1,384,1536]{3,2,1,0:T(8,128)(2,1)} %stream_in.1, f32[1536]{0:T(1024)} %gate_in.1, bf16[96,1536]{1,0:T(8,128)(2,1)} %w_in.1, ...), custom_call_target="tpu_custom_call" | custom-call | tf_op jit(solution)/shard_map/block/pallas_call | solution.py:365
  78.4 2.4 %copy.9 = bf16[1,1,384,1536]{3,2,1,0:T(8,128)(2,1)} copy(bf16[1,1,384,1536]{3,2,1,0:T(8,128)(2,1)} %block.1) | data formatting | bytes 2359296
